TPU v7x, 32 devices: a whole 2x2x4 slice. The times are simulated.
32 devices in a mesh: gx: 4 (over y, x), gy: 2 (over core), gz: 4 (over z).
Axes of the slice: x: 2, y: 2, z: 4, core: 2. Of those that a mesh axis runs over, the one named last changes fastest.
Arguments:
- local_schur: bfloat16 [4, 2, 4, 882, 882], P('gx', 'gy', 'gz'), may hold values from -15 to 20, as said below
- schur_inverse: bfloat16 [4, 2, 4, 882, 882], P('gx', 'gy', 'gz'), may hold values from -1.5 to 2, as said below
- load_terms: bfloat16 [4, 2, 4, 6, 147, 128], P('gx', 'gy', 'gz'), may hold values from -6 to 6
- corner_basis: float32 [4, 2, 4, 8, 882], P('gx', 'gy', 'gz'), may hold values from -0.21875 to 0.21875
- corner_map: int32 [4, 2, 4, 8], replicated, may hold values from 0 to 9, as said below
- coarse_inverse: bfloat16 [9, 9], replicated, may hold values from -6 to 8, as said below
Outputs:
- solution: float32 [4, 2, 4, 6, 147, 128], P('gx', 'gy', 'gz')
Inputs may be any that keep to these rules, and one draw needn't show every extreme that they name: `local_schur`: each 882 x 882 matrix is symmetric positive definite. `schur_inverse`: each 882 x 882 matrix is symmetric positive definite. `coarse_inverse`: symmetric positive definite. `corner_map`: corner k of subdomain (a, b, c) is the lattice point (a + k // 4, b + (k // 2) % 2, c + k % 2) of the (5) x (3) x (5) corner lattice; points on the lattice's outside have the number 9, interior points are numbered 0 to 8 by a permutation, so subdomains that meet at a point give it the same number.
All inputs are finite; a program needn't handle non-finite values.
Results may differ from a plain program's by a relative error of at most 0.0022.
Values may be sent and summed in bfloat16 or wider, within the bound.
A program may use at most 64 MiB of HBM per device.

v0:
```python
import functools
import math

import jax
import jax.numpy as jnp
from jax import lax
from jax.experimental import pallas as pl
from jax.experimental.pallas import tpu as pltpu
from jax.sharding import PartitionSpec as P

ITERS = 3
FACES = 6
AXES = ("gx", "gy", "gz")
PANEL = 8
VMEM_BYTES = 50 * 1024 * 1024
HIGHEST = lax.Precision.HIGHEST
MESH = pl.DeviceIdType.MESH


def dot(left, right, dims=((1,), (0,)), precision=None):
    return lax.dot_general(
        left, right, (dims, ((), ())), precision=precision, preferred_element_type=jnp.float32
    )


def split2(values):
    high = values.astype(jnp.bfloat16)
    low = (values - high.astype(jnp.float32)).astype(jnp.bfloat16)
    return high, low


def split3(values):
    first = values.astype(jnp.bfloat16).astype(jnp.float32)
    rest = values - first
    second = rest.astype(jnp.bfloat16).astype(jnp.float32)
    return first, second, rest - second


def group_index(group):
    index = 0
    for axis in group:
        index = index * lax.axis_size(axis) + lax.axis_index(axis)
    return index


def group_size(group):
    return math.prod(lax.axis_size(axis) for axis in group)


def group_device(group, index):
    where = {}
    for axis in reversed(group):
        size = lax.axis_size(axis)
        where[axis] = index % size
        index = index // size
    return where


def live_face(face):
    axis = AXES[face // 2]
    place = lax.axis_index(axis)
    return place < lax.axis_size(axis) - 1 if face % 2 else place > 0


def across(face):
    axis = AXES[face // 2]
    return {axis: lax.axis_index(axis) + (1 if face % 2 else -1)}


def face_copy(face, source, target, send_sems, recv_sems):
    return pltpu.make_async_remote_copy(
        src_ref=source.at[face],
        dst_ref=target.at[face ^ 1],
        send_sem=send_sems.at[face],
        recv_sem=recv_sems.at[face ^ 1],
        device_id=across(face),
        device_id_type=MESH,
    )


def send_face(face, *refs):
    @pl.when(live_face(face))
    def _():
        face_copy(face, *refs).start()


def wait_face(face, source, target, send_sems, recv_sems):
    @pl.when(live_face(face))
    def _():
        copy = pltpu.make_async_remote_copy(
            src_ref=source.at[face],
            dst_ref=target.at[face],
            send_sem=send_sems.at[face],
            recv_sem=recv_sems.at[face],
            device_id=across(face),
            device_id_type=MESH,
        )
        copy.wait_recv()
        copy.wait_send()


def exchange_kernel(blocks, load, near_blocks, near_load, block_send, block_recv, load_send, load_recv):
    barrier = pltpu.get_barrier_semaphore()
    for face in range(FACES):
        @pl.when(live_face(face))
        def _():
            pl.semaphore_signal(barrier, inc=1, device_id=across(face), device_id_type=MESH)
    pl.semaphore_wait(barrier, sum(live_face(face).astype(jnp.int32) for face in range(FACES)))
    for face in range(FACES):
        send_face(face, blocks, near_blocks, block_send, block_recv)
    for face in range(FACES):
        send_face(face, load, near_load, load_send, load_recv)
    for face in range(FACES):
        wait_face(face, blocks, near_blocks, block_send, block_recv)
    for face in range(FACES):
        wait_face(face, load, near_load, load_send, load_recv)


def inverse_kernel(size, live, blocks, near, basis, hot, d_high, d_low, t_high, t_low, gather, work):
    padded = work.shape[1]
    rows = lax.broadcasted_iota(jnp.int32, (padded, padded), 0)
    cols = lax.broadcasted_iota(jnp.int32, (padded, padded), 1)
    unit = jnp.where((rows == cols) & (rows >= size), 1.0, 0.0)
    for face in range(FACES):
        block = blocks[face].astype(jnp.float32)[:padded, :padded]
        other = near[face].astype(jnp.float32)[:padded, :padded]
        block = block + jnp.where(live[face] > 0, other, 0.0)
        work[face] = jnp.where((rows < size) & (cols < size), block, unit)
    lane = lax.broadcasted_iota(jnp.int32, (PANEL, padded), 1)
    row = lax.broadcasted_iota(jnp.int32, (PANEL, padded), 0)
    for start in range(0, padded, PANEL):
        panels = [work[face, start : start + PANEL, :] for face in range(FACES)]
        swept = list(panels)
        for step in range(PANEL):
            pivot = start + step
            for face in range(FACES):
                held = swept[face]
                column = held[:, pivot : pivot + 1]
                scale = 1.0 / held[step : step + 1, pivot : pivot + 1]
                at_pivot = lane == pivot
                line = jnp.where(at_pivot[:1], scale, held[step : step + 1, :] * scale)
                kept = jnp.where(at_pivot, 0.0, held)
                swept[face] = jnp.where(row == step, line, kept - column * line)
        inside = (lane >= start) & (lane < start + PANEL)
        column_inside = (cols >= start) & (cols < start + PANEL)
        for face in range(FACES):
            signed = jnp.where(inside, -swept[face], swept[face])
            u0, u1, u2 = split3(panels[face])
            w0, w1, w2 = split3(signed)
            left = jnp.concatenate([u0, u0, u1, u1, u0, u2], axis=0).astype(jnp.bfloat16)
            right = jnp.concatenate([w0, w1, w0, w1, w2, w0], axis=0).astype(jnp.bfloat16)
            change = dot(left, right, ((0,), (0,)))
            work[face] = jnp.where(column_inside, 0.0, work[face]) - change
            work[face, start : start + PANEL, :] = signed
    for face in range(FACES):
        inverse = -work[face][:size, :size]
        block = blocks[face].astype(jnp.float32)[:size, :size].astype(jnp.bfloat16)
        parts = [part.astype(jnp.bfloat16) for part in split3(inverse)]
        deluxe = dot(parts[0], block) + (dot(parts[1], block) + dot(parts[2], block))
        turned = dot(block, parts[0]) + (dot(block, parts[1]) + dot(block, parts[2]))
        d_high[face], d_low[face] = split2(deluxe)
        corner = dot(hot[...], basis[face], precision=HIGHEST)
        rows_up = dot(corner, turned, precision=HIGHEST)
        gather[face] = rows_up
        top = rows_up.shape[0]
        t_high[face, :top], t_low[face, :top] = split2(rows_up)
        t_high[face, top:], t_low[face, top:] = split2(turned)


def cg_kernel(
    groups, schur, inverse, load, near_load, d_high, d_low, t_high, t_low, gather, coarse, out,
    near_gather, own, near, wide_own, wide_near, residual, direction, flat, wide_sums, thin_sums,
    halo_send, halo_recv, gather_send, gather_recv, sum_send, sum_recv,
):
    size = load.shape[1]
    cases = load.shape[2]
    sizes = [group_size(group) for group in groups]
    bases = [sum(sizes[:stage]) for stage in range(len(groups))]
    places = [group_index(group) for group in groups]
    live = [live_face(face) for face in range(FACES)]

    barrier = pltpu.get_barrier_semaphore()
    for stage, group in enumerate(groups):
        for away in range(1, sizes[stage]):
            peer = (places[stage] + away) % sizes[stage]
            pl.semaphore_signal(barrier, inc=1, device_id=group_device(group, peer), device_id_type=MESH)
    pl.semaphore_wait(barrier, sum(sizes) - len(groups))

    def part_copy(sums, call, stage, slot, peer, sem_slot):
        place = bases[stage] + slot
        return pltpu.make_async_remote_copy(
            src_ref=sums.at[place],
            dst_ref=sums.at[place],
            send_sem=sum_send.at[call, bases[stage] + peer],
            recv_sem=sum_recv.at[call, bases[stage] + sem_slot],
            device_id=group_device(groups[stage], peer),
            device_id_type=MESH,
        )

    def start_sum(sums, call, stage, value):
        me = places[stage]
        sums[bases[stage] + me] = value
        for away in range(1, sizes[stage]):
            peer = (me + away) % sizes[stage]
            part_copy(sums, call, stage, me, peer, me).start()

    def end_sum(sums, call, stage):
        me = places[stage]
        for away in range(1, sizes[stage]):
            peer = (me + away) % sizes[stage]
            part_copy(sums, call, stage, peer, peer, peer).wait_recv()
        total = sums[bases[stage]]
        for slot in range(1, sizes[stage]):
            total = total + sums[bases[stage] + slot]
        return total

    def finish_sum(sums, call):
        total = end_sum(sums, call, 0)
        for stage in range(1, len(groups)):
            start_sum(sums, call, stage, total)
            total = end_sum(sums, call, stage)
        return total

    def drain_sum(sums, call):
        for stage in range(len(groups)):
            me = places[stage]
            for away in range(1, sizes[stage]):
                peer = (me + away) % sizes[stage]
                part_copy(sums, call, stage, me, peer, me).wait_send()

    def rows_of(face):
        return slice(face * size, (face + 1) * size)

    for face in range(FACES):
        send_face(face, gather, near_gather, gather_send, gather_recv)
    for face in range(FACES):
        total = load[face].astype(jnp.float32) + near_load[face].astype(jnp.float32)
        residual[face] = jnp.where(live[face], total, 0.0)

    wide_rows = wide_sums.shape[2]
    last_row = lax.broadcasted_iota(jnp.int32, (wide_rows, cases), 0) == wide_rows - 1

    for turn in range(ITERS):
        wide = wide_sums.at[turn]
        corner_part = jnp.zeros((wide_rows, cases), jnp.float32)
        for face in range(FACES):
            held = residual[face]
            high, low = split2(held)
            both = dot(t_high[face], high) + (dot(t_low[face], high) + dot(t_high[face], low))
            corner_part = corner_part + both[:wide_rows]
            flat[rows_of(face), :] = both[wide_rows:]
        scaled = flat[...]
        local_value = dot(inverse[...], scaled.astype(jnp.bfloat16))
        rho_part = jnp.sum(scaled * local_value, axis=0, keepdims=True)
        start_sum(wide, 2 * turn, 0, corner_part + jnp.where(last_row, rho_part, 0.0))
        flat[...] = local_value
        halo = (own.at[turn], near.at[turn], halo_send.at[2 * turn], halo_recv.at[2 * turn])
        for face in range(FACES):
            high, low = split2(flat[rows_of(face), :])
            value = dot(d_high[face], high) + (dot(d_low[face], high) + dot(d_high[face], low))
            own[turn, face] = value
            send_face(face, *halo)
        total = finish_sum(wide, 2 * turn)
        coarse_value = dot(coarse[...], total.astype(jnp.bfloat16))
        rho_next = jnp.sum(jnp.where(last_row, total, total * coarse_value), axis=0, keepdims=True)
        value_high, value_low = split2(coarse_value)
        if turn == 0:
            for face in range(FACES):
                wait_face(face, gather, near_gather, gather_send, gather_recv)
        for face in range(FACES):
            wait_face(face, *halo)
            high, low = split2(gather[face] + near_gather[face])
            step_z = own[turn, face] + near[turn, face] + dot(high, value_high, ((0,), (0,)))
            step_z = step_z + (dot(low, value_high, ((0,), (0,))) + dot(high, value_low, ((0,), (0,))))
            if turn > 0:
                step_z = step_z + rho_next / rho * direction[face]
            step_z = jnp.where(live[face], step_z, 0.0)
            direction[face] = step_z
            flat[rows_of(face), :] = step_z
        rho = rho_next
        thin = thin_sums.at[turn]
        wide_direction = flat[...]
        image = dot(schur[...], wide_direction.astype(jnp.bfloat16))
        bend = jnp.sum(wide_direction * image, axis=0, keepdims=True)
        start_sum(thin, 2 * turn + 1, 0, bend)
        final = turn + 1 == ITERS
        if not final:
            flat[...] = image
            halo = (
                wide_own.at[turn], wide_near.at[turn],
                halo_send.at[2 * turn + 1], halo_recv.at[2 * turn + 1],
            )
            for face in range(FACES):
                wide_own[turn, face] = flat[rows_of(face), :]
                send_face(face, *halo)
        step_size = rho / finish_sum(thin, 2 * turn + 1)
        for face in range(FACES):
            move = step_size * direction[face]
            out[face] = move if turn == 0 else out[face] + move
            if not final:
                wait_face(face, *halo)
                joined = wide_own[turn, face] + wide_near[turn, face]
                residual[face] = jnp.where(live[face], residual[face] - step_size * joined, 0.0)
    for turn in range(ITERS):
        drain_sum(wide_sums.at[turn], 2 * turn)
        drain_sum(thin_sums.at[turn], 2 * turn + 1)


def vmem(count):
    return [pl.BlockSpec(memory_space=pltpu.VMEM)] * count


def params(collective_id=None):
    if collective_id is None:
        return pltpu.CompilerParams(vmem_limit_bytes=VMEM_BYTES)
    return pltpu.CompilerParams(
        vmem_limit_bytes=VMEM_BYTES, collective_id=collective_id, has_side_effects=True
    )


def local(local_schur, schur_inverse, load_terms, corner_basis, corner_map, coarse_inverse):
    size, cases = load_terms.shape[4:]
    order = FACES * size
    matrix = local_schur.reshape(order, order)
    inverse = schur_inverse.reshape(order, order)
    load = load_terms.reshape(FACES, size, cases)
    places = [lax.axis_index(axis) for axis in AXES]
    counts = [lax.axis_size(axis) for axis in AXES]
    corners = coarse_inverse.shape[0]
    wide_rows = (corners + 1 + 15) // 16 * 16
    own_corners = corner_map[places[0], places[1], places[2]]
    own_corners = jnp.where(own_corners < corners, own_corners, -1)
    hot = (lax.broadcasted_iota(jnp.int32, (wide_rows, 8), 0) == own_corners[None, :]).astype(jnp.float32)
    basis = corner_basis.reshape(8, FACES, size).transpose(1, 0, 2)
    coarse = jnp.pad(coarse_inverse, ((0, wide_rows - corners), (0, wide_rows - corners)))
    flags = []
    for axis in range(3):
        flags.append(places[axis] > 0)
        flags.append(places[axis] < counts[axis] - 1)
    flags = jnp.stack(flags).astype(jnp.int32)

    tall = (size + 15) // 16 * 16
    broad = (size + 127) // 128 * 128
    padded = (size + PANEL - 1) // PANEL * PANEL
    margins = ((0, tall - size), (0, broad - size))
    blocks = jnp.stack(
        [
            jnp.pad(matrix[f * size : (f + 1) * size, f * size : (f + 1) * size], margins)
            for f in range(FACES)
        ]
    )
    tall_load = jnp.pad(load, ((0, 0), (0, tall - size), (0, 0)))
    near_blocks, near_load = pl.pallas_call(
        exchange_kernel,
        out_shape=[
            jax.ShapeDtypeStruct(blocks.shape, blocks.dtype),
            jax.ShapeDtypeStruct(tall_load.shape, tall_load.dtype),
        ],
        in_specs=vmem(2),
        out_specs=vmem(2),
        scratch_shapes=[pltpu.SemaphoreType.DMA((FACES,))] * 4,
        compiler_params=params(0),
        name="exchange",
    )(blocks, tall_load)

    square = jax.ShapeDtypeStruct((FACES, size, size), jnp.bfloat16)
    factors = pl.pallas_call(
        functools.partial(inverse_kernel, size),
        out_shape=[square] * 2
        + [jax.ShapeDtypeStruct((FACES, wide_rows + size, size), jnp.bfloat16)] * 2
        + [
            jax.ShapeDtypeStruct((FACES, wide_rows, size), jnp.float32),
        ],
        in_specs=[pl.BlockSpec(memory_space=pltpu.SMEM)] + vmem(4),
        out_specs=vmem(5),
        scratch_shapes=[pltpu.VMEM((FACES, padded, padded), jnp.float32)],
        compiler_params=params(),
        name="deluxe",
    )(flags, blocks, near_blocks, basis, hot)

    groups = (("gx", "gy"), ("gz",)) if math.prod(counts) <= 32 else (("gx",), ("gy",), ("gz",))
    slots = sum(group_size(group) for group in groups)
    halos = 2 * ITERS - 1
    face_shape = (FACES, size, cases)
    dma = pltpu.SemaphoreType.DMA
    result = pl.pallas_call(
        functools.partial(cg_kernel, groups),
        out_shape=jax.ShapeDtypeStruct(face_shape, jnp.float32),
        in_specs=vmem(10),
        out_specs=vmem(1)[0],
        scratch_shapes=[
            pltpu.VMEM((FACES, wide_rows, size), jnp.float32),
            pltpu.VMEM((ITERS,) + face_shape, jnp.float32),
            pltpu.VMEM((ITERS,) + face_shape, jnp.float32),
            pltpu.VMEM((ITERS - 1,) + face_shape, jnp.float32),
            pltpu.VMEM((ITERS - 1,) + face_shape, jnp.float32),
            pltpu.VMEM(face_shape, jnp.float32),
            pltpu.VMEM(face_shape, jnp.float32),
            pltpu.VMEM((order, cases), jnp.float32),
            pltpu.VMEM((ITERS, slots, wide_rows, cases), jnp.float32),
            pltpu.VMEM((ITERS, slots, 1, cases), jnp.float32),
            dma((halos, FACES)),
            dma((halos, FACES)),
            dma((FACES,)),
            dma((FACES,)),
            dma((2 * ITERS, slots)),
            dma((2 * ITERS, slots)),
        ],
        compiler_params=params(1),
        name="iterate",
    )(matrix, inverse, load, near_load[:, :size], *factors, coarse)
    return result.reshape(1, 1, 1, FACES, size, cases)


def solution(mesh):
    placed = (
        P("gx", "gy", "gz", None, None),
        P("gx", "gy", "gz", None, None),
        P("gx", "gy", "gz", None, None, None),
        P("gx", "gy", "gz", None, None),
        P(),
        P(),
    )
    return jax.shard_map(
        local,
        mesh=mesh,
        in_specs=placed,
        out_specs=P("gx", "gy", "gz", None, None, None),
        check_vma=False,
    )
```

profile of v0, /device:TPU:0, one launch (start us, length us, event | category | flops | bytes accessed | tf_op | source)
XLA Modules:
  0.0 92.9 jit_solution(3718038608636053904)
XLA Ops:
  0.0 0.0 copy-start
  0.0 0.0 copy-start.1
  0.0 1.5 %fusion.1 = (bf16[147,147]{1,0:T(8,128)(2,1)S(1)}, bf16[147,147]{1,0:T(8,128)(2,1)S(1)}, bf16[147,147]{1,0:T(8,128)(2,1)S(1)}, bf16[147,147]{1,0:T(8,128)(2,1)S(...) fusion(bf16[882,882]{1,0:T(8,128)(2,1)} %bitcast.33), kind=kLoop, calls=%fused_computation.10 | loop fusion | bytes 518616 | tf_op jit(solution)/shard_map/slice | solution.py:348
  1.6 0.0 copy-start.2
  1.6 0.0 copy-done
  1.7 10.1 %exchange.1 = (bf16[6,160,256]{2,1,0:T(8,128)(2,1)S(1)}, bf16[6,160,128]{2,1,0:T(8,128)(2,1)S(1)}) custom-call(bf16[6,160,256]{2,1,0:T(8,128)(2,1)S(1)} %bitcast_dynamic-update-slice_fusion.blocks, bf16[6,160,128]{2,1,0:T(8,128)(2,1)S(1)} %pad.33.load), custom_call_target="tpu_custom_call" | custom-call | tf_op jit(solution)/shard_map/exchange/pallas_call | solution.py:353
  11.8 0.1 stack.55
  11.9 0.0 copy-done.1
  11.9 0.1 reshape.27
  12.0 0.7 compare_select_fusion
  12.7 19.1 %deluxe.1 = (bf16[6,147,147]{2,1,0:T(8,128)(2,1)S(1)}, bf16[6,147,147]{2,1,0:T(8,128)(2,1)S(1)}, bf16[6,163,147]{2,1,0:T(8,128)(2,1)S(1)}, bf16[6,163,147]{2,1,0:T(8,128)(2,1)S(1)}, f32[6,16,147]{2,1,0:T(8,128)S(1)}) custom-call(s32[6]{0:T(128)S(1)} %convert_element_type.17.live, bf16[6,160,256]{2,1,0:T(8,128)(2,1)S(1)} %bitcast_dynamic-update-slice_fusion.blocks, ...), custom_call_target="tpu_custom_call" | custom-call | tf_op jit(solution)/shard_map/deluxe/pallas_call | solution.py:367
  31.8 0.0 copy-done.2
  31.8 59.9 %iterate.1 = f32[6,147,128]{2,1,0:T(8,128)S(1)} custom-call(bf16[882,882]{1,0:T(8,128)(2,1)} %bitcast.34, bf16[882,882]{1,0:T(8,128)(2,1)} %bitcast.35, bf16[6,147,128]{2,1,0:T(8,128)(2,1)S(1)} %bitcast.31, bf16[6,147,128]{2,1,0:T(8,128)(2,1)S(1)} %slice.27.near_load, bf16[6,147,147]{2,1,0:T(8,128)(2,1)S(1)} %get-tuple-element.14.d_high, ...), custom_call_target="tpu_custom_call" | custom-call | tf_op jit(solution)/shard_map/iterate/pallas_call | solution.py:386
  91.7 1.2 %copy.9 = f32[1,1,1,6,147,128]{5,2,4,3,1,0:T(1,128)} copy(f32[1,1,1,6,147,128]{5,4,3,2,1,0:T(8,128)S(1)} %bitcast.29) | data formatting | bytes 903168 | tf_op jit(solution)/shard_map/reshape | solution.py:412
  (12 shorter events, 0.2 us)
Async XLA Ops:
  0.0 1.6 %copy-start = (bf16[1,1,1,6,147,128]{5,4,3,2,1,0:T(8,128)(2,1)S(1)}, bf16[1,1,1,6,147,128]{5,4,3,2,1,0:T(8,128)(2,1)}, u32[]{:S(2)}) copy-start(bf16[1,1,1,6,147,128]{5,4,3,2,1,0:T(8,128)(2,1)} %param.8) | copy-start | bytes 677380
  0.0 11.9 %copy-start.1 = (f32[1,1,1,8,882]{4,3,2,1,0:T(8,128)S(1)}, f32[1,1,1,8,882]{4,3,2,1,0:T(8,128)}, u32[]{:S(2)}) copy-start(f32[1,1,1,8,882]{4,3,2,1,0:T(8,128)} %param.9) | copy-start | bytes 84676
  1.6 30.2 %copy-start.2 = (bf16[9,9]{1,0:T(8,128)(2,1)S(1)}, bf16[9,9]{1,0:T(8,128)(2,1)}, u32[]{:S(2)}) copy-start(bf16[9,9]{1,0:T(8,128)(2,1)} %param.11) | copy-start | bytes 490
where the time goes:
time: 93.1 us; the launch traced here: 92.9 us
  Pallas kernels  89 us (96%)
  local copies, waits for them, and re-layouts  3.06 us (3%)
    pallas_call x1, Pallas kernels, local(): pl.pallas_call(functools.partial(cg_kernel, groups), out_shape=jax.ShapeD...  59.9 us
    pallas_call x1, Pallas kernels, local(): pl.pallas_call(functools.partial(inverse_kernel, size), out_shape=[square...  19.1 us
    pallas_call x1, Pallas kernels, local(): pl.pallas_call(exchange_kernel, out_shape=[jax.ShapeDtypeStruct(blocks.sh...  10.1 us

commit v1 on v0

--- a/solution.py
+++ b/solution.py
@@ -131,16 +131,22 @@
     for start in range(0, padded, PANEL):
         panels = [work[face, start : start + PANEL, :] for face in range(FACES)]
         swept = list(panels)
-        for step in range(PANEL):
+        for step in range(0, PANEL, 2):
             pivot = start + step
+            first, second = lane[:1] == pivot, lane[:1] == pivot + 1
+            both = (lane == pivot) | (lane == pivot + 1)
             for face in range(FACES):
                 held = swept[face]
-                column = held[:, pivot : pivot + 1]
-                scale = 1.0 / held[step : step + 1, pivot : pivot + 1]
-                at_pivot = lane == pivot
-                line = jnp.where(at_pivot[:1], scale, held[step : step + 1, :] * scale)
-                kept = jnp.where(at_pivot, 0.0, held)
-                swept[face] = jnp.where(row == step, line, kept - column * line)
+                left = jnp.broadcast_to(held[:, pivot : pivot + 1], held.shape)
+                right = jnp.broadcast_to(held[:, pivot + 1 : pivot + 2], held.shape)
+                a, b = left[step : step + 1], left[step + 1 : step + 2]
+                c = right[step + 1 : step + 2]
+                scale = 1.0 / (a * c - b * b)
+                upper = jnp.where(both[:1], jnp.where(first, 1.0, 0.0), held[step : step + 1])
+                lower = jnp.where(both[:1], jnp.where(second, 1.0, 0.0), held[step + 1 : step + 2])
+                upper, lower = (c * upper - b * lower) * scale, (a * lower - b * upper) * scale
+                kept = jnp.where(both, 0.0, held) - left * upper - right * lower
+                swept[face] = jnp.where(row == step, upper, jnp.where(row == step + 1, lower, kept))
         inside = (lane >= start) & (lane < start + PANEL)
         column_inside = (cols >= start) & (cols < start + PANEL)
         for face in range(FACES):

time: 93.1 us -> 88.1 us (0.946)
  Pallas kernels: 89 us -> 84 us
    pallas_call x1, Pallas kernels: 19.1 us -> 14.1 us  [local(): pl.pallas_call(functools.partial(inverse_kernel, size), out_shape=[square...]
where the time goes in v1:
time: 88.1 us; the launch traced here: 87.9 us
  Pallas kernels  84 us (95%)
  local copies, waits for them, and re-layouts  3.06 us (3%)
    pallas_call x1, Pallas kernels, local(): pl.pallas_call(functools.partial(cg_kernel, groups), out_shape=jax.ShapeD...  59.8 us
    pallas_call x1, Pallas kernels, local(): pl.pallas_call(functools.partial(inverse_kernel, size), out_shape=[square...  14.1 us
    pallas_call x1, Pallas kernels, local(): pl.pallas_call(exchange_kernel, out_shape=[jax.ShapeDtypeStruct(blocks.sh...  10.1 us

profile of v1, /device:TPU:0, one launch (start us, length us, event | category | flops | bytes accessed | tf_op | source)
XLA Modules:
  0.0 87.9 jit_solution(15109051299387138795)
XLA Ops:
  0.0 0.0 copy-start
  0.0 0.0 copy-start.1
  0.0 1.5 %fusion.1 = (bf16[147,147]{1,0:T(8,128)(2,1)S(1)}, bf16[147,147]{1,0:T(8,128)(2,1)S(1)}, bf16[147,147]{1,0:T(8,128)(2,1)S(1)}, bf16[147,147]{1,0:T(8,128)(2,1)S(...) fusion(bf16[882,882]{1,0:T(8,128)(2,1)} %bitcast.33), kind=kLoop, calls=%fused_computation.10 | loop fusion | bytes 518616 | tf_op jit(solution)/shard_map/slice | solution.py:354
  1.6 0.0 copy-start.2
  1.6 0.0 copy-done
  1.7 10.1 %exchange.1 = (bf16[6,160,256]{2,1,0:T(8,128)(2,1)S(1)}, bf16[6,160,128]{2,1,0:T(8,128)(2,1)S(1)}) custom-call(bf16[6,160,256]{2,1,0:T(8,128)(2,1)S(1)} %bitcast_dynamic-update-slice_fusion.blocks, bf16[6,160,128]{2,1,0:T(8,128)(2,1)S(1)} %pad.33.load), custom_call_target="tpu_custom_call" | custom-call | tf_op jit(solution)/shard_map/exchange/pallas_call | solution.py:359
  11.8 0.1 stack.55
  11.9 0.0 copy-done.1
  11.9 0.1 reshape.27
  12.0 0.7 compare_select_fusion
  12.7 14.1 %deluxe.1 = (bf16[6,147,147]{2,1,0:T(8,128)(2,1)S(1)}, bf16[6,147,147]{2,1,0:T(8,128)(2,1)S(1)}, bf16[6,163,147]{2,1,0:T(8,128)(2,1)S(1)}, bf16[6,163,147]{2,1,0:T(8,128)(2,1)S(1)}, f32[6,16,147]{2,1,0:T(8,128)S(1)}) custom-call(s32[6]{0:T(128)S(1)} %convert_element_type.17.live, bf16[6,160,256]{2,1,0:T(8,128)(2,1)S(1)} %bitcast_dynamic-update-slice_fusion.blocks, ...), custom_call_target="tpu_custom_call" | custom-call | tf_op jit(solution)/shard_map/deluxe/pallas_call | solution.py:373
  26.8 0.0 copy-done.2
  26.8 59.8 %iterate.1 = f32[6,147,128]{2,1,0:T(8,128)S(1)} custom-call(bf16[882,882]{1,0:T(8,128)(2,1)} %bitcast.34, bf16[882,882]{1,0:T(8,128)(2,1)} %bitcast.35, bf16[6,147,128]{2,1,0:T(8,128)(2,1)S(1)} %bitcast.31, bf16[6,147,128]{2,1,0:T(8,128)(2,1)S(1)} %slice.27.near_load, bf16[6,147,147]{2,1,0:T(8,128)(2,1)S(1)} %get-tuple-element.14.d_high, ...), custom_call_target="tpu_custom_call" | custom-call | tf_op jit(solution)/shard_map/iterate/pallas_call | solution.py:392
  86.7 1.2 %copy.9 = f32[1,1,1,6,147,128]{5,2,4,3,1,0:T(1,128)} copy(f32[1,1,1,6,147,128]{5,4,3,2,1,0:T(8,128)S(1)} %bitcast.29) | data formatting | bytes 903168 | tf_op jit(solution)/shard_map/reshape | solution.py:418
  (12 shorter events, 0.2 us)
Async XLA Ops:
  0.0 1.6 %copy-start = (bf16[1,1,1,6,147,128]{5,4,3,2,1,0:T(8,128)(2,1)S(1)}, bf16[1,1,1,6,147,128]{5,4,3,2,1,0:T(8,128)(2,1)}, u32[]{:S(2)}) copy-start(bf16[1,1,1,6,147,128]{5,4,3,2,1,0:T(8,128)(2,1)} %param.8) | copy-start | bytes 677380
  0.0 11.9 %copy-start.1 = (f32[1,1,1,8,882]{4,3,2,1,0:T(8,128)S(1)}, f32[1,1,1,8,882]{4,3,2,1,0:T(8,128)}, u32[]{:S(2)}) copy-start(f32[1,1,1,8,882]{4,3,2,1,0:T(8,128)} %param.9) | copy-start | bytes 84676
  1.6 25.2 %copy-start.2 = (bf16[9,9]{1,0:T(8,128)(2,1)S(1)}, bf16[9,9]{1,0:T(8,128)(2,1)}, u32[]{:S(2)}) copy-start(bf16[9,9]{1,0:T(8,128)(2,1)} %param.11) | copy-start | bytes 490
